TPU v7x, 32 devices: a whole 2x2x4 slice. The times are simulated.
32 devices in a mesh: gx: 4 (over y, x), gy: 8 (over z, core).
Axes of the slice: x: 2, y: 2, z: 4, core: 2. Of those that a mesh axis runs over, the one named last changes fastest.
Arguments:
- electric: float32 [3, 64, 64, 256], P(None, 'gx', 'gy'), may hold values from -1.5 to 1.5
- magnetic: float32 [3, 64, 64, 256], P(None, 'gx', 'gy'), may hold values from -6 to 6
- material: int32 [64, 64, 256], P('gx', 'gy'), may hold values from 0 to 7
- permittivity: float32 [8], replicated, may hold values from 1 to 4
- conductivity: float32 [8], replicated, may hold values from 0.01 to 1
Outputs:
- advanced_electric: float32 [3, 64, 64, 256], P(None, 'gx', 'gy')
- advanced_magnetic: float32 [3, 64, 64, 256], P(None, 'gx', 'gy')
All inputs are finite; a program needn't handle non-finite values.
Results may differ from a plain program's by a relative error of at most 0.0003.
Values sent between devices are 32-bit elements; how exact they have to be, the bound alone decides.
A program may use at most 64 MiB of HBM per device.

v0:
```python
import functools

import jax
import jax.numpy as jnp
from jax import lax
from jax.experimental import pallas as pl
from jax.experimental.pallas import tpu as pltpu
from jax.sharding import PartitionSpec as P

half_step = 12.0
MESH = pl.DeviceIdType.MESH


def strides(length):
    found, stride = [], 1
    while stride < length:
        found.append(stride)
        stride *= 2
    return found


def roll(v, by, axis):
    return pltpu.roll(v, by % v.shape[axis], axis)


def position(shape, axis):
    return lax.broadcasted_iota(jnp.int32, shape, axis)


def reduce_matrix(diagonal, above):
    length, levels = diagonal.shape[0], []
    for stride in strides(length):
        inverse = 1.0 / diagonal
        below = roll(above, stride, 0)
        from_below = -below * roll(inverse, stride, 0)
        from_above = -above * roll(inverse, -stride, 0)
        levels.append((stride, from_below, from_above))
        diagonal = diagonal + from_below * below + from_above * above
        if 2 * stride < length:
            above = from_above * roll(above, -stride, 0)
    return levels, 1.0 / diagonal


def reduce_source(source, system):
    levels, inverse = system
    for stride, from_below, from_above in levels:
        source = source + from_below * roll(source, stride, 0) + from_above * roll(source, -stride, 0)
    return source * inverse


def eliminate(diagonals):
    pivots = [1.0 / diagonals[0]]
    for diagonal in diagonals[1:]:
        pivots.append(1.0 / (diagonal - pivots[-1]))
    return pivots


def back(rows, pivots):
    result = [rows[-1]]
    for row, pivot in zip(rows[-2::-1], pivots[-2::-1]):
        result.append(row + pivot * result[-1])
    return result[::-1]


def solve(rows, pivots):
    done = [rows[0] * pivots[0]]
    for row, pivot in zip(rows[1:], pivots[1:]):
        done.append((row + done[-1]) * pivot)
    return back(done, pivots)


def corners(pivots):
    done = [pivots[0]]
    for pivot in pivots[1:]:
        done.append(done[-1] * pivot)
    last = [pivots[-1]]
    for pivot in pivots[-2::-1]:
        last.append(last[-1] * pivot)
    return back(done, pivots), last[::-1]


def dot(left, right):
    terms = [a * b for a, b in zip(left, right)]
    while len(terms) > 1:
        terms = [sum(terms[i:i + 2][1:], terms[i]) for i in range(0, len(terms), 2)]
    return terms[0]


def sweep_matrix(first, cross, last):
    gain, pivots, mults, gains = jnp.zeros_like(first[0]), [], [], []
    for k in range(len(first)):
        pivot = 1.0 / (1.0 - first[k] * gain)
        mult = cross[k] * pivot
        pivots.append(pivot)
        mults.append(mult)
        gains.append(gain)
        gain = last[k] + mult * gain * cross[k]
    gains.append(gain)
    return pivots, mults, gains


def sweep(first, cross, matrix, w_first, w_last):
    pivots, mults, gains = matrix
    count = len(first)
    sums = [jnp.zeros_like(w_first[0])]
    for k in range(count):
        sums.append(w_last[k] + mults[k] * (sums[k] + gains[k] * w_first[k]))
    p, q = [None] * count, [None] * (count + 1)
    q[count] = jnp.zeros_like(w_first[0])
    for k in reversed(range(count)):
        p[k] = sums[k + 1] + gains[k + 1] * q[k + 1]
        q[k] = pivots[k] * (w_first[k] + first[k] * sums[k] + cross[k] * q[k + 1])
    return p, q


def kernel(
    nx, ny,
    e_in, h_in, mat_in, eps_in, sig_in, out,
    e_ref, h_ref, mat_ref, eps_ref, sig_ref,
    halo_xs, halo_ys, halo_xr, halo_yr,
    xm_s, xm_r, xa_s, xa_r, ym_s, ym_r, ya_s, ya_r, yb_s, yb_r,
    p_ref, q_ref, pq_ref, plane_ref, yt_ref, zt_ref, out_ref,
    load, store, halo_send, halo_recv, x_send, x_recv, y_send, y_recv,
):
    cx, cy, cz = mat_ref.shape
    rows = cx // ny
    lanes = yt_ref.shape[2]
    ix, iy = lax.axis_index("gx"), lax.axis_index("gy")
    x_others = [lax.rem(ix + d, nx) for d in range(1, nx)]
    y_others = [lax.rem(iy + d, ny) for d in range(1, ny)]

    loads = [
        pltpu.make_async_copy(src, dst, load.at[k])
        for k, (src, dst) in enumerate(
            [(mat_in, mat_ref), (eps_in, eps_ref), (sig_in, sig_ref), (e_in, e_ref), (h_in, h_ref)]
        )
    ]
    for copy in loads:
        copy.start()
    halo_xr[...] = jnp.zeros_like(halo_xr)
    halo_yr[...] = jnp.zeros_like(halo_yr)
    barrier = pltpu.get_barrier_semaphore()
    for other in x_others:
        pl.semaphore_signal(barrier, inc=1, device_id=(other, iy), device_id_type=MESH)
    for other in y_others:
        pl.semaphore_signal(barrier, inc=1, device_id=(ix, other), device_id_type=MESH)
    for copy in loads[:3]:
        copy.wait()
    material = mat_ref[...]
    excess = jnp.zeros(material.shape, jnp.float32)
    carry = jnp.zeros(material.shape, jnp.float32)
    for row in range(eps_ref.shape[0]):
        permit = eps_ref[row] * (1.0 / half_step)
        lossy = sig_ref[row] * 0.5
        chosen = material == row
        excess = jnp.where(chosen, (permit + lossy) * (1.0 / half_step), excess)
        carry = jnp.where(chosen, (permit - lossy) * (1.0 / half_step), carry)
    for copy in loads[3:]:
        copy.wait()

    halo_xs[0] = e_ref[1, 0]
    halo_xs[1] = h_ref[2, cx - 1]
    halo_ys[0] = e_ref[2, :, 0, :]
    halo_ys[1] = h_ref[0, :, cy - 1, :]
    pl.semaphore_wait(barrier, nx + ny - 2)

    def halo(src, dst, k, to):
        return pltpu.make_async_remote_copy(
            src_ref=src, dst_ref=dst, send_sem=halo_send.at[k], recv_sem=halo_recv.at[k],
            device_id=to, device_id_type=MESH,
        )

    halos = [
        (halo(halo_xs.at[0], halo_xr.at[0], 0, (lax.rem(ix + nx - 1, nx), iy)), ix > 0, ix < nx - 1),
        (halo(halo_xs.at[1], halo_xr.at[1], 1, (lax.rem(ix + 1, nx), iy)), ix < nx - 1, ix > 0),
        (halo(halo_ys.at[0], halo_yr.at[0], 2, (ix, lax.rem(iy + ny - 1, ny))), iy > 0, iy < ny - 1),
        (halo(halo_ys.at[1], halo_yr.at[1], 3, (ix, lax.rem(iy + 1, ny))), iy < ny - 1, iy > 0),
    ]
    for copy, sends, _ in halos:
        pl.when(sends)(copy.start)

    def emit(k, value):
        out_ref[k] = value
        pltpu.make_async_copy(out_ref.at[k], out.at[k], store.at[k]).start()

    def x_copy(src, dst, phase, to):
        return pltpu.make_async_remote_copy(
            src_ref=src, dst_ref=dst, send_sem=x_send.at[phase], recv_sem=x_recv.at[phase],
            device_id=(to, iy), device_id_type=MESH,
        )

    def x_start(src, buffer, phase):
        for other in x_others:
            x_copy(src, buffer.at[ix], phase, other).start()
        buffer[ix] = src[...]

    def x_all(buffer, phase):
        part = buffer.at[pl.ds(0, nx - 1)]
        return x_copy(part, part, phase, x_others[0])

    def y_copy(src, dst, phase, to):
        return pltpu.make_async_remote_copy(
            src_ref=src, dst_ref=dst, send_sem=y_send.at[phase], recv_sem=y_recv.at[phase],
            device_id=(ix, to), device_id_type=MESH,
        )

    def y_start(src, buffer, phase):
        for other in y_others:
            y_copy(src.at[other], buffer.at[iy], phase, other).start()
        buffer[iy] = src[iy]

    def y_all(buffer, phase):
        part = buffer.at[pl.ds(0, ny - 1)]
        return y_copy(part, part, phase, y_others[0])

    def y_pack(buffer, planes):
        for i, plane in enumerate(planes):
            plane_ref[i] = plane
        for k in range(ny):
            for i in range(len(planes)):
                buffer[k, i * rows:(i + 1) * rows, :] = plane_ref[i, k * rows:(k + 1) * rows, :]

    def y_store(v):
        flat = v.reshape(cx * cy, cz)
        for half in range(cz // lanes):
            yt_ref[half] = flat[:, half * lanes:(half + 1) * lanes]

    def y_row(k):
        return jnp.concatenate(
            [yt_ref[half, pl.ds(k, cx, stride=cy), :] for half in range(cz // lanes)], axis=1
        )

    def y_rows(v):
        y_store(v)
        return [y_row(k) for k in range(cy)]

    def y_natural(planes):
        for k, plane in enumerate(planes):
            for half in range(cz // lanes):
                yt_ref[half, pl.ds(k, cx, stride=cy), :] = plane[:, half * lanes:(half + 1) * lanes]
        return jnp.concatenate(
            [yt_ref[half] for half in range(cz // lanes)], axis=1
        ).reshape(cx, cy, cz)

    at_y, at_z = position(material.shape, 1), position(material.shape, 2)
    diagonal = excess + 2.0

    diagonals = y_rows(diagonal)
    diagonals[0] = jnp.where(iy == 0, diagonals[0] - 1.0, diagonals[0])
    pivots_y = eliminate(diagonals)
    left_y, right_y = corners(pivots_y)
    y_pack(ym_s, [left_y[0], right_y[0], right_y[-1]])
    y_start(ym_s, ym_r, 0)
    diagonals = [diagonal[k] for k in range(cx)]
    diagonals[0] = jnp.where(ix == 0, diagonals[0] - 1.0, diagonals[0])
    pivots_x = eliminate(diagonals)
    left_x, right_x = corners(pivots_x)
    xm_s[0] = left_x[0]
    xm_s[1] = right_x[0]
    xm_s[2] = right_x[-1]
    x_start(xm_s, xm_r, 0)

    block = zt_ref.shape[0] // 16
    count = cz // block

    def z_rows(v):
        zt_ref[...] = v.reshape(cx * cy, cz).T
        return [zt_ref[pl.ds(k, count, stride=block), :] for k in range(block)]

    def z_solve(v):
        planes = z_rows(v)
        inner, edge = planes[:-1], planes[-1]
        edge = edge + dot(right_z, inner) + jnp.where(
            at_block == count - 1, 0.0, roll(dot(left_z, inner), -1, 0)
        )
        edge = reduce_source(edge, system_z)
        inner[0] = inner[0] + jnp.where(at_block == 0, 0.0, roll(edge, 1, 0))
        inner[-1] = inner[-1] + edge
        for k, plane in enumerate(solve(inner, pivots_z) + [edge]):
            zt_ref[pl.ds(k, count, stride=block), :] = plane
        return zt_ref[...].T.reshape(cx, cy, cz)

    def forward_z(v):
        return jnp.where(at_z == cz - 1, 0.0, roll(v, -1, 2)) - v

    def backward_z(v):
        return v - jnp.where(at_z == 0, 0.0, roll(v, 1, 2))

    def forward_y(v, upper):
        return jnp.where(at_y == cy - 1, upper, roll(v, -1, 1)) - v

    def backward_y(v, lower):
        return v - jnp.where(at_y == 0, lower, roll(v, 1, 1))

    def forward_x(v, upper):
        return jnp.concatenate([v[1:], upper], axis=0) - v

    def backward_x(v, lower):
        return v - jnp.concatenate([lower, v[:-1]], axis=0)

    no_x = jnp.zeros((1, cy, cz), jnp.float32)
    scale = 1.0 / half_step

    def x_send_block(source, absorbed, sign, phase):
        planes = [source[k] for k in range(cx)]
        xa_s[phase - 1, 0] = dot(left_x, planes)
        xa_s[phase - 1, 1] = dot(right_x, planes) - (sign * scale) * absorbed[cx - 1]
        x_start(xa_s.at[phase - 1], xa_r.at[phase - 1], phase)
        return planes

    def y_send_block(source, absorbed, sign, phase):
        y_store(absorbed)
        last = y_row(cy - 1)
        planes = y_rows(source)
        y_pack(
            ya_s.at[phase - 1], [dot(left_y, planes), dot(right_y, planes) - (sign * scale) * last]
        )
        y_start(ya_s.at[phase - 1], ya_r.at[phase - 1], phase)
        return planes

    def x_finish(planes, phase, matrix):
        first, cross, terms = matrix
        x_all(xa_r.at[phase - 1], phase).wait_recv()
        p, q = sweep(
            first, cross, terms,
            [xa_r[phase - 1, k, 0] for k in range(nx)], [xa_r[phase - 1, k, 1] for k in range(nx)],
        )
        p_ref[0] = jnp.zeros_like(p[0])
        for k in range(nx):
            p_ref[k + 1] = p[k]
            q_ref[k] = q[k]
        q_ref[nx] = q[nx]
        left, right = p_ref[ix], q_ref[ix + 1]
        planes = [planes[0] + left] + planes[1:-1] + [planes[-1] + right]
        return jnp.stack(solve(planes, pivots_x)), left[None], right[None]

    def y_reduce(phase, matrix):
        first, cross, terms = matrix
        buffer = ya_r.at[phase - 1]
        y_all(buffer, phase).wait_recv()
        p, q = sweep(
            first, cross, terms,
            [buffer[k, 0:rows, :] for k in range(ny)], [buffer[k, rows:2 * rows, :] for k in range(ny)],
        )
        out = yb_s.at[phase - 1]
        for k in range(ny):
            out[k, 0:rows, :] = p[k - 1] if k else jnp.zeros_like(p[0])
            out[k, rows:2 * rows, :] = q[k + 1]
        y_start(out, yb_r.at[phase - 1], phase + 2)

    def y_finish(planes, phase):
        buffer = yb_r.at[phase - 1]
        y_all(buffer, phase + 2).wait_recv()
        for k in range(ny):
            for i in range(2):
                plane_ref[i, k * rows:(k + 1) * rows, :] = buffer[k, i * rows:(i + 1) * rows, :]
        left, right = plane_ref[0], plane_ref[1]
        pq_ref[:, 0, :] = left
        pq_ref[:, 1, :] = right
        planes = [planes[0] + left] + planes[1:-1] + [planes[-1] + right]
        return y_natural(solve(planes, pivots_y)), pq_ref[:, 0:1, :], pq_ref[:, 1:2, :]

    interim_y = h_ref[1] - half_step * forward_z(e_ref[0])
    for copy, _, receives in halos:
        pl.when(receives)(copy.wait_recv)
    interim_z = h_ref[2] - half_step * forward_x(e_ref[1], halo_xr[0:1])
    rows_center_x = y_send_block(
        carry * e_ref[0] + scale * (backward_y(interim_z, 0.0) - backward_z(h_ref[1])),
        interim_z, 1.0, 1,
    )
    pq_ref[:, 0, :] = halo_yr[0]
    pq_ref[:, 1, :] = halo_yr[1]
    ez_above, hx_below = pq_ref[:, 0:1, :], pq_ref[:, 1:2, :]
    rows_center_z = x_send_block(
        carry * e_ref[2] + scale * (backward_x(interim_y, no_x) - backward_y(h_ref[0], hx_below)),
        interim_y, 1.0, 1,
    )
    y_all(ym_r, 0).wait_recv()
    first_y = [ym_r[k, 0:rows, :] for k in range(ny)]
    cross_y = [ym_r[k, rows:2 * rows, :] for k in range(ny)]
    last_y = [ym_r[k, 2 * rows:3 * rows, :] for k in range(ny)]
    matrix_y = (first_y, cross_y, sweep_matrix(first_y, cross_y, last_y))
    x_all(xm_r, 0).wait_recv()
    first_x = [xm_r[k, 0] for k in range(nx)]
    cross_x = [xm_r[k, 1] for k in range(nx)]
    matrix_x = (first_x, cross_x, sweep_matrix(first_x, cross_x, [xm_r[k, 2] for k in range(nx)]))

    diagonals = z_rows(jnp.where(at_z == 0, diagonal - 1.0, diagonal))
    at_block = position(diagonals[0].shape, 0)
    pivots_z = eliminate(diagonals[:-1])
    left_z, right_z = corners(pivots_z)
    inside = at_block < count - 1
    system_z = reduce_matrix(
        diagonals[-1] - right_z[-1] - jnp.where(inside, roll(left_z[0], -1, 0), 0.0),
        jnp.where(inside, -roll(right_z[0], -1, 0), 0.0),
    )
    interim_x = h_ref[0] - half_step * forward_y(e_ref[2], ez_above)
    center_y = z_solve(
        carry * e_ref[1] + scale * (backward_z(interim_x) - backward_x(h_ref[2], halo_xr[1:2]))
    )
    curl_x = half_step * forward_z(center_y)
    middle_x = interim_x + curl_x
    second_x = middle_x + curl_x

    y_reduce(1, matrix_y)
    center_z, left, right = x_finish(rows_center_z, 1, matrix_x)
    curl_y = half_step * forward_x(center_z, right)
    middle_y = interim_y + curl_y
    second_y = middle_y + curl_y
    middle_y_below = jnp.where(ix > 0, half_step * (center_z[0:1] - left), 0.0)
    rows_final_z = y_send_block(
        carry * center_z + scale * (backward_x(middle_y, middle_y_below) - backward_y(second_x, 0.0)),
        second_x, -1.0, 2,
    )
    center_x, left, right = y_finish(rows_center_x, 1)
    curl_z = half_step * forward_y(center_x, right)
    middle_z = interim_z + curl_z
    second_z = middle_z + curl_z
    rows_final_y = x_send_block(
        carry * center_y + scale * (backward_z(middle_x) - backward_x(second_z, no_x)),
        second_z, -1.0, 2,
    )
    middle_z_below = jnp.where(iy > 0, half_step * (center_x[:, 0:1, :] - left), 0.0)
    y_reduce(2, matrix_y)
    final_x = z_solve(
        carry * center_x + scale * (backward_y(middle_z, middle_z_below) - backward_z(second_y))
    )
    emit(0, final_x)
    emit(4, second_y - half_step * forward_z(final_x))
    final_y, _, right = x_finish(rows_final_y, 2, matrix_x)
    emit(1, final_y)
    emit(5, second_z - half_step * forward_x(final_y, right))
    final_z, _, right = y_finish(rows_final_z, 2)
    emit(2, final_z)
    emit(3, second_x - half_step * forward_y(final_z, right))

    for k in range(6):
        pltpu.make_async_copy(out_ref.at[k], out.at[k], store.at[k]).wait()
    for copy, sends, _ in halos:
        pl.when(sends)(copy.wait_send)
    for phase, buffer in enumerate([xm_r, xa_r.at[0], xa_r.at[1]]):
        x_all(buffer, phase).wait_send()
    for phase, buffer in enumerate([ym_r, ya_r.at[0], ya_r.at[1], yb_r.at[0], yb_r.at[1]]):
        y_all(buffer, phase).wait_send()


def per_device(nx, ny, electric, magnetic, material, permittivity, conductivity):
    cx, cy, cz = material.shape
    rows = cx // ny
    cell = (cx, cy, cz)
    vmem, smem = pltpu.VMEM, pltpu.SMEM
    in_hbm = pl.BlockSpec(memory_space=pltpu.HBM)

    def f32(*shape):
        return vmem(shape, jnp.float32)

    dma = pltpu.SemaphoreType.DMA
    advanced = pl.pallas_call(
        functools.partial(kernel, nx, ny),
        out_shape=jax.ShapeDtypeStruct((6,) + cell, jnp.float32),
        in_specs=[in_hbm] * 5,
        out_specs=in_hbm,
        scratch_shapes=[
            f32(3, *cell), f32(3, *cell), vmem(cell, jnp.int32),
            smem(permittivity.shape, jnp.float32), smem(conductivity.shape, jnp.float32),
            f32(2, cy, cz), f32(2, cx, cz), f32(2, cy, cz), f32(2, cx, cz),
            f32(3, cy, cz), f32(nx, 3, cy, cz), f32(2, 2, cy, cz), f32(2, nx, 2, cy, cz),
            f32(ny, 3 * rows, cz), f32(ny, 3 * rows, cz),
            f32(2, ny, 2 * rows, cz), f32(2, ny, 2 * rows, cz),
            f32(2, ny, 2 * rows, cz), f32(2, ny, 2 * rows, cz),
            f32(nx + 1, cy, cz), f32(nx + 1, cy, cz), f32(*cell), f32(3, cx, cz),
            f32(cz // 128, cx * cy, 128), f32(cz, cx * cy), f32(6, *cell),
            dma((5,)), dma((6,)), dma((4,)), dma((4,)), dma((3,)), dma((3,)), dma((5,)), dma((5,)),
        ],
        compiler_params=pltpu.CompilerParams(
            collective_id=0, has_side_effects=True, vmem_limit_bytes=62 * 1024 * 1024
        ),
    )(electric, magnetic, material, permittivity, conductivity)
    return advanced[:3], advanced[3:]


def solution(mesh):
    nx, ny = mesh.shape["gx"], mesh.shape["gy"]
    return jax.shard_map(
        functools.partial(per_device, nx, ny),
        mesh=mesh,
        in_specs=(
            P(None, "gx", "gy", None),
            P(None, "gx", "gy", None),
            P("gx", "gy", None),
            P(),
            P(),
        ),
        out_specs=(P(None, "gx", "gy", None), P(None, "gx", "gy", None)),
        check_vma=False,
    )
```

profile of v0, /device:TPU:0, one launch (start us, length us, event | category | flops | bytes accessed | tf_op | source)
XLA Modules:
  0.0 23.3 jit_solution(6170896915776918453)
XLA Ops:
  0.6 20.6 %shard_map.68 = f32[6,16,8,256]{3,2,1,0:T(8,128)} custom-call(f32[3,16,8,256]{3,2,1,0:T(8,128)} %e_in.1, f32[3,16,8,256]{3,2,1,0:T(8,128)} %h_in.1, s32[16,8,256]{2,1,0:T(8,128)} %mat_in.1, f32[8]{0:T(128)} %eps_in.1, f32[8]{0:T(128)} %sig_in.1), custom_call_target="tpu_custom_call" | custom-call | tf_op jit(solution)/shard_map/pallas_call | solution.py:458
  21.3 2.1 %fusion = (f32[3,16,8,256]{3,2,1,0:T(8,128)}, f32[3,16,8,256]{3,2,1,0:T(8,128)}) fusion(f32[6,16,8,256]{3,2,1,0:T(8,128)} %shard_map.68), kind=kLoop, calls=%fused_computation | loop fusion | bytes 1572864 | tf_op jit(solution)/shard_map/slice | solution.py:479
where the time goes:
time: 23.5 us; the launch traced here: 23.3 us
  Pallas kernels  20.6 us (88%)
  local copies, waits for them, and re-layouts  2.08 us (9%)
  between operations  0.64 us (3%)
    pallas_call x1, Pallas kernels, per_device(): pl.pallas_call(functools.partial(kernel, nx, ny), out_shape=jax.ShapeDtyp...  20.6 us
    slice x1, local copies, waits for them, and re-layouts, per_device(): return (advanced[:3], advanced[3:])  2.08 us

commit v1 on v0

--- a/solution.py
+++ b/solution.py
@@ -48,11 +48,13 @@
     return source * inverse
 
 
-def eliminate(diagonals):
-    pivots = [1.0 / diagonals[0]]
-    for diagonal in diagonals[1:]:
-        pivots.append(1.0 / (diagonal - pivots[-1]))
-    return pivots
+def eliminate(systems):
+    found = [[1.0 / diagonals[0]] for diagonals in systems]
+    for k in range(1, max(len(diagonals) for diagonals in systems)):
+        for diagonals, pivots in zip(systems, found):
+            if k < len(diagonals):
+                pivots.append(1.0 / (diagonals[k] - pivots[-1]))
+    return found
 
 
 def back(rows, pivots):
@@ -113,19 +115,25 @@
     return p, q
 
 
+def solvers(ny):
+    return (ny // 2, ny // 4) if ny % 4 == 0 else (ny, 0)
+
+
 def kernel(
     nx, ny,
-    e_in, h_in, mat_in, eps_in, sig_in, out,
+    e_in, h_in, mat_in, eps_in, sig_in, e_out, h_out,
     e_ref, h_ref, mat_ref, eps_ref, sig_ref,
     halo_xs, halo_ys, halo_xr, halo_yr,
-    xm_s, xm_r, xa_s, xa_r, ym_s, ym_r, ya_s, ya_r, yb_s, yb_r,
+    xm_s, xm_r, xa_s, xa_r, ym_s, ym_r, ya_s, ya_r, yb_s, yb_r, sweep_ref,
     p_ref, q_ref, pq_ref, plane_ref, yt_ref, zt_ref, out_ref,
     load, store, halo_send, halo_recv, x_send, x_recv, y_send, y_recv,
 ):
     cx, cy, cz = mat_ref.shape
-    rows = cx // ny
+    ns, s0 = solvers(ny)
+    rows = cx // ns
     lanes = yt_ref.shape[2]
     ix, iy = lax.axis_index("gx"), lax.axis_index("gy")
+    solving = (iy >= s0) & (iy < s0 + ns)
     x_others = [lax.rem(ix + d, nx) for d in range(1, nx)]
     y_others = [lax.rem(iy + d, ny) for d in range(1, ny)]
 
@@ -144,8 +152,30 @@
         pl.semaphore_signal(barrier, inc=1, device_id=(other, iy), device_id_type=MESH)
     for other in y_others:
         pl.semaphore_signal(barrier, inc=1, device_id=(ix, other), device_id_type=MESH)
-    for copy in loads[:3]:
+    for copy in loads:
         copy.wait()
+
+    halo_xs[0] = e_ref[1, 0]
+    halo_xs[1] = h_ref[2, cx - 1]
+    halo_ys[0] = e_ref[2, :, 0, :]
+    halo_ys[1] = h_ref[0, :, cy - 1, :]
+    pl.semaphore_wait(barrier, nx + ny - 2)
+
+    def halo(src, dst, k, to):
+        return pltpu.make_async_remote_copy(
+            src_ref=src, dst_ref=dst, send_sem=halo_send.at[k], recv_sem=halo_recv.at[k],
+            device_id=to, device_id_type=MESH,
+        )
+
+    halos = [
+        (halo(halo_xs.at[0], halo_xr.at[0], 0, (lax.rem(ix + nx - 1, nx), iy)), ix > 0, ix < nx - 1),
+        (halo(halo_xs.at[1], halo_xr.at[1], 1, (lax.rem(ix + 1, nx), iy)), ix < nx - 1, ix > 0),
+        (halo(halo_ys.at[0], halo_yr.at[0], 2, (ix, lax.rem(iy + ny - 1, ny))), iy > 0, iy < ny - 1),
+        (halo(halo_ys.at[1], halo_yr.at[1], 3, (ix, lax.rem(iy + 1, ny))), iy < ny - 1, iy > 0),
+    ]
+    for copy, sends, _ in halos:
+        pl.when(sends)(copy.start)
+
     material = mat_ref[...]
     excess = jnp.zeros(material.shape, jnp.float32)
     carry = jnp.zeros(material.shape, jnp.float32)
@@ -155,33 +185,12 @@
         chosen = material == row
         excess = jnp.where(chosen, (permit + lossy) * (1.0 / half_step), excess)
         carry = jnp.where(chosen, (permit - lossy) * (1.0 / half_step), carry)
-    for copy in loads[3:]:
-        copy.wait()
-
-    halo_xs[0] = e_ref[1, 0]
-    halo_xs[1] = h_ref[2, cx - 1]
-    halo_ys[0] = e_ref[2, :, 0, :]
-    halo_ys[1] = h_ref[0, :, cy - 1, :]
-    pl.semaphore_wait(barrier, nx + ny - 2)
-
-    def halo(src, dst, k, to):
-        return pltpu.make_async_remote_copy(
-            src_ref=src, dst_ref=dst, send_sem=halo_send.at[k], recv_sem=halo_recv.at[k],
-            device_id=to, device_id_type=MESH,
-        )
-
-    halos = [
-        (halo(halo_xs.at[0], halo_xr.at[0], 0, (lax.rem(ix + nx - 1, nx), iy)), ix > 0, ix < nx - 1),
-        (halo(halo_xs.at[1], halo_xr.at[1], 1, (lax.rem(ix + 1, nx), iy)), ix < nx - 1, ix > 0),
-        (halo(halo_ys.at[0], halo_yr.at[0], 2, (ix, lax.rem(iy + ny - 1, ny))), iy > 0, iy < ny - 1),
-        (halo(halo_ys.at[1], halo_yr.at[1], 3, (ix, lax.rem(iy + 1, ny))), iy < ny - 1, iy > 0),
-    ]
-    for copy, sends, _ in halos:
-        pl.when(sends)(copy.start)
+
+    out = [e_out.at[k] for k in range(3)] + [h_out.at[k] for k in range(3)]
 
     def emit(k, value):
         out_ref[k] = value
-        pltpu.make_async_copy(out_ref.at[k], out.at[k], store.at[k]).start()
+        pltpu.make_async_copy(out_ref.at[k], out[k], store.at[k]).start()
 
     def x_copy(src, dst, phase, to):
         return pltpu.make_async_remote_copy(
@@ -204,19 +213,35 @@
             device_id=(ix, to), device_id_type=MESH,
         )
 
-    def y_start(src, buffer, phase):
+    def y_gather(src, buffer, phase):
+        for d in range(ns):
+            s = lax.rem(iy + d, ns)
+            copy = y_copy(src.at[s], buffer.at[iy], phase, s0 + s)
+            pl.when(iy != s0 + s)(copy.start)
+
+        @pl.when(solving)
+        def _():
+            buffer[iy] = src[iy - s0]
+
+    def y_scatter(src, buffer, phase):
         for other in y_others:
-            y_copy(src.at[other], buffer.at[iy], phase, other).start()
-        buffer[iy] = src[iy]
-
-    def y_all(buffer, phase):
-        part = buffer.at[pl.ds(0, ny - 1)]
+            y_copy(src.at[other], buffer.at[iy - s0], phase, other).start()
+        buffer[iy - s0] = src[iy]
+
+    def y_part(buffer, count, phase):
+        part = buffer.at[pl.ds(0, count)]
         return y_copy(part, part, phase, y_others[0])
+
+    def y_from_solvers(buffer, phase, send):
+        for when, count in ((solving, ns - 1), (jnp.logical_not(solving), ns)):
+            if count:
+                copy = y_part(buffer, count, phase)
+                pl.when(when)(copy.wait_send if send else copy.wait_recv)
 
     def y_pack(buffer, planes):
         for i, plane in enumerate(planes):
             plane_ref[i] = plane
-        for k in range(ny):
+        for k in range(ns):
             for i in range(len(planes)):
                 buffer[k, i * rows:(i + 1) * rows, :] = plane_ref[i, k * rows:(k + 1) * rows, :]
 
@@ -245,27 +270,34 @@
     at_y, at_z = position(material.shape, 1), position(material.shape, 2)
     diagonal = excess + 2.0
 
-    diagonals = y_rows(diagonal)
-    diagonals[0] = jnp.where(iy == 0, diagonals[0] - 1.0, diagonals[0])
-    pivots_y = eliminate(diagonals)
+    block = zt_ref.shape[0] // 16
+    count = cz // block
+
+    def z_rows(v):
+        zt_ref[...] = v.reshape(cx * cy, cz).T
+        return [zt_ref[pl.ds(k, count, stride=block), :] for k in range(block)]
+
+    lines_x = [diagonal[k] for k in range(cx)]
+    lines_x[0] = jnp.where(ix == 0, lines_x[0] - 1.0, lines_x[0])
+    lines_y = y_rows(diagonal)
+    lines_y[0] = jnp.where(iy == 0, lines_y[0] - 1.0, lines_y[0])
+    lines_z = z_rows(jnp.where(at_z == 0, diagonal - 1.0, diagonal))
+    pivots_x, pivots_y, pivots_z = eliminate([lines_x, lines_y, lines_z[:-1]])
     left_y, right_y = corners(pivots_y)
+    left_x, right_x = corners(pivots_x)
+    left_z, right_z = corners(pivots_z)
     y_pack(ym_s, [left_y[0], right_y[0], right_y[-1]])
-    y_start(ym_s, ym_r, 0)
-    diagonals = [diagonal[k] for k in range(cx)]
-    diagonals[0] = jnp.where(ix == 0, diagonals[0] - 1.0, diagonals[0])
-    pivots_x = eliminate(diagonals)
-    left_x, right_x = corners(pivots_x)
+    y_gather(ym_s, ym_r, 0)
     xm_s[0] = left_x[0]
     xm_s[1] = right_x[0]
     xm_s[2] = right_x[-1]
     x_start(xm_s, xm_r, 0)
-
-    block = zt_ref.shape[0] // 16
-    count = cz // block
-
-    def z_rows(v):
-        zt_ref[...] = v.reshape(cx * cy, cz).T
-        return [zt_ref[pl.ds(k, count, stride=block), :] for k in range(block)]
+    at_block = position(lines_z[0].shape, 0)
+    inside = at_block < count - 1
+    system_z = reduce_matrix(
+        lines_z[-1] - right_z[-1] - jnp.where(inside, roll(left_z[0], -1, 0), 0.0),
+        jnp.where(inside, -roll(right_z[0], -1, 0), 0.0),
+    )
 
     def z_solve(v):
         planes = z_rows(v)
@@ -315,7 +347,7 @@
         y_pack(
             ya_s.at[phase - 1], [dot(left_y, planes), dot(right_y, planes) - (sign * scale) * last]
         )
-        y_start(ya_s.at[phase - 1], ya_r.at[phase - 1], phase)
+        y_gather(ya_s.at[phase - 1], ya_r.at[phase - 1], phase)
         return planes
 
     def x_finish(planes, phase, matrix):
@@ -334,24 +366,28 @@
         planes = [planes[0] + left] + planes[1:-1] + [planes[-1] + right]
         return jnp.stack(solve(planes, pivots_x)), left[None], right[None]
 
-    def y_reduce(phase, matrix):
-        first, cross, terms = matrix
-        buffer = ya_r.at[phase - 1]
-        y_all(buffer, phase).wait_recv()
-        p, q = sweep(
-            first, cross, terms,
-            [buffer[k, 0:rows, :] for k in range(ny)], [buffer[k, rows:2 * rows, :] for k in range(ny)],
-        )
-        out = yb_s.at[phase - 1]
-        for k in range(ny):
-            out[k, 0:rows, :] = p[k - 1] if k else jnp.zeros_like(p[0])
-            out[k, rows:2 * rows, :] = q[k + 1]
-        y_start(out, yb_r.at[phase - 1], phase + 2)
+    def y_reduce(phase):
+        @pl.when(solving)
+        def _():
+            buffer = ya_r.at[phase - 1]
+            y_part(buffer, ny - 1, phase).wait_recv()
+            p, q = sweep(
+                [ym_r[k, 0:rows, :] for k in range(ny)],
+                [ym_r[k, rows:2 * rows, :] for k in range(ny)],
+                [[sweep_ref[i, k] for k in range(ny + 1 if i == 2 else ny)] for i in range(3)],
+                [buffer[k, 0:rows, :] for k in range(ny)],
+                [buffer[k, rows:2 * rows, :] for k in range(ny)],
+            )
+            out = yb_s.at[phase - 1]
+            for k in range(ny):
+                out[k, 0:rows, :] = p[k - 1] if k else jnp.zeros_like(p[0])
+                out[k, rows:2 * rows, :] = q[k + 1]
+            y_scatter(out, yb_r.at[phase - 1], phase + 2)
 
     def y_finish(planes, phase):
         buffer = yb_r.at[phase - 1]
-        y_all(buffer, phase + 2).wait_recv()
-        for k in range(ny):
+        y_from_solvers(buffer, phase + 2, False)
+        for k in range(ns):
             for i in range(2):
                 plane_ref[i, k * rows:(k + 1) * rows, :] = buffer[k, i * rows:(i + 1) * rows, :]
         left, right = plane_ref[0], plane_ref[1]
@@ -375,25 +411,21 @@
         carry * e_ref[2] + scale * (backward_x(interim_y, no_x) - backward_y(h_ref[0], hx_below)),
         interim_y, 1.0, 1,
     )
-    y_all(ym_r, 0).wait_recv()
-    first_y = [ym_r[k, 0:rows, :] for k in range(ny)]
-    cross_y = [ym_r[k, rows:2 * rows, :] for k in range(ny)]
-    last_y = [ym_r[k, 2 * rows:3 * rows, :] for k in range(ny)]
-    matrix_y = (first_y, cross_y, sweep_matrix(first_y, cross_y, last_y))
+    @pl.when(solving)
+    def _():
+        y_part(ym_r, ny - 1, 0).wait_recv()
+        terms = sweep_matrix(
+            *[[ym_r[k, i * rows:(i + 1) * rows, :] for k in range(ny)] for i in range(3)]
+        )
+        for i, planes in enumerate(terms):
+            for k, plane in enumerate(planes):
+                sweep_ref[i, k] = plane
+
     x_all(xm_r, 0).wait_recv()
     first_x = [xm_r[k, 0] for k in range(nx)]
     cross_x = [xm_r[k, 1] for k in range(nx)]
     matrix_x = (first_x, cross_x, sweep_matrix(first_x, cross_x, [xm_r[k, 2] for k in range(nx)]))
 
-    diagonals = z_rows(jnp.where(at_z == 0, diagonal - 1.0, diagonal))
-    at_block = position(diagonals[0].shape, 0)
-    pivots_z = eliminate(diagonals[:-1])
-    left_z, right_z = corners(pivots_z)
-    inside = at_block < count - 1
-    system_z = reduce_matrix(
-        diagonals[-1] - right_z[-1] - jnp.where(inside, roll(left_z[0], -1, 0), 0.0),
-        jnp.where(inside, -roll(right_z[0], -1, 0), 0.0),
-    )
     interim_x = h_ref[0] - half_step * forward_y(e_ref[2], ez_above)
     center_y = z_solve(
         carry * e_ref[1] + scale * (backward_z(interim_x) - backward_x(h_ref[2], halo_xr[1:2]))
@@ -402,7 +434,7 @@
     middle_x = interim_x + curl_x
     second_x = middle_x + curl_x
 
-    y_reduce(1, matrix_y)
+    y_reduce(1)
     center_z, left, right = x_finish(rows_center_z, 1, matrix_x)
     curl_y = half_step * forward_x(center_z, right)
     middle_y = interim_y + curl_y
@@ -421,7 +453,7 @@
         second_z, -1.0, 2,
     )
     middle_z_below = jnp.where(iy > 0, half_step * (center_x[:, 0:1, :] - left), 0.0)
-    y_reduce(2, matrix_y)
+    y_reduce(2)
     final_x = z_solve(
         carry * center_x + scale * (backward_y(middle_z, middle_z_below) - backward_z(second_y))
     )
@@ -435,18 +467,24 @@
     emit(3, second_x - half_step * forward_y(final_z, right))
 
     for k in range(6):
-        pltpu.make_async_copy(out_ref.at[k], out.at[k], store.at[k]).wait()
+        pltpu.make_async_copy(out_ref.at[k], out[k], store.at[k]).wait()
     for copy, sends, _ in halos:
         pl.when(sends)(copy.wait_send)
     for phase, buffer in enumerate([xm_r, xa_r.at[0], xa_r.at[1]]):
         x_all(buffer, phase).wait_send()
-    for phase, buffer in enumerate([ym_r, ya_r.at[0], ya_r.at[1], yb_r.at[0], yb_r.at[1]]):
-        y_all(buffer, phase).wait_send()
+    for phase, buffer in enumerate([ym_s, ya_s.at[0], ya_s.at[1]]):
+        y_from_solvers(buffer, phase, True)
+
+    @pl.when(solving)
+    def _():
+        for phase in (3, 4):
+            y_part(yb_s.at[phase - 3], ny - 1, phase).wait_send()
 
 
 def per_device(nx, ny, electric, magnetic, material, permittivity, conductivity):
     cx, cy, cz = material.shape
-    rows = cx // ny
+    ns, _ = solvers(ny)
+    rows = cx // ns
     cell = (cx, cy, cz)
     vmem, smem = pltpu.VMEM, pltpu.SMEM
     in_hbm = pl.BlockSpec(memory_space=pltpu.HBM)
@@ -457,17 +495,17 @@
     dma = pltpu.SemaphoreType.DMA
     advanced = pl.pallas_call(
         functools.partial(kernel, nx, ny),
-        out_shape=jax.ShapeDtypeStruct((6,) + cell, jnp.float32),
+        out_shape=(jax.ShapeDtypeStruct((3,) + cell, jnp.float32),) * 2,
         in_specs=[in_hbm] * 5,
-        out_specs=in_hbm,
+        out_specs=(in_hbm,) * 2,
         scratch_shapes=[
             f32(3, *cell), f32(3, *cell), vmem(cell, jnp.int32),
             smem(permittivity.shape, jnp.float32), smem(conductivity.shape, jnp.float32),
             f32(2, cy, cz), f32(2, cx, cz), f32(2, cy, cz), f32(2, cx, cz),
             f32(3, cy, cz), f32(nx, 3, cy, cz), f32(2, 2, cy, cz), f32(2, nx, 2, cy, cz),
-            f32(ny, 3 * rows, cz), f32(ny, 3 * rows, cz),
-            f32(2, ny, 2 * rows, cz), f32(2, ny, 2 * rows, cz),
-            f32(2, ny, 2 * rows, cz), f32(2, ny, 2 * rows, cz),
+            f32(ns, 3 * rows, cz), f32(ny, 3 * rows, cz),
+            f32(2, ns, 2 * rows, cz), f32(2, ny, 2 * rows, cz),
+            f32(2, ny, 2 * rows, cz), f32(2, ns, 2 * rows, cz), f32(3, ny + 1, rows, cz),
             f32(nx + 1, cy, cz), f32(nx + 1, cy, cz), f32(*cell), f32(3, cx, cz),
             f32(cz // 128, cx * cy, 128), f32(cz, cx * cy), f32(6, *cell),
             dma((5,)), dma((6,)), dma((4,)), dma((4,)), dma((3,)), dma((3,)), dma((5,)), dma((5,)),
@@ -476,7 +514,7 @@
             collective_id=0, has_side_effects=True, vmem_limit_bytes=62 * 1024 * 1024
         ),
     )(electric, magnetic, material, permittivity, conductivity)
-    return advanced[:3], advanced[3:]
+    return advanced
 
 
 def solution(mesh):

time: 23.5 us -> 23.2 us (0.987)
  Pallas kernels: 20.6 us -> 19.9 us
  local copies, waits for them, and re-layouts: 2.08 us -> 2.57 us
    unnamed x0 -> x4, local copies, waits for them, and re-layouts: none -> 2.57 us
    slice x1 -> x0, local copies, waits for them, and re-layouts: 2.08 us -> none  [per_device(): return (advanced[:3], advanced[3:])]
    pallas_call x1, Pallas kernels: 20.6 us -> 19.9 us  [per_device(): pl.pallas_call(functools.partial(kernel, nx, ny), out_shape=(jax.ShapeDty...]
where the time goes in v1:
time: 23.2 us; the launch traced here: 23.1 us
  Pallas kernels  19.9 us (86%)
  local copies, waits for them, and re-layouts  2.57 us (11%)
  between operations  0.65 us (3%)
    pallas_call x1, Pallas kernels, per_device(): pl.pallas_call(functools.partial(kernel, nx, ny), out_shape=(jax.ShapeDty...  19.9 us
    unnamed x4, local copies, waits for them, and re-layouts  2.57 us

profile of v1, /device:TPU:0, one launch (start us, length us, event | category | flops | bytes accessed | tf_op | source)
XLA Modules:
  0.0 23.1 jit_solution(16793475482112205581)
XLA Ops:
  0.6 19.9 %shard_map.68 = (f32[3,16,8,256]{3,2,1,0:T(8,128)}, f32[3,16,8,256]{3,2,1,0:T(8,128)}) custom-call(f32[3,16,8,256]{3,2,1,0:T(8,128)} %e_in.1, f32[3,16,8,256]{3,2,1,0:T(8,128)} %h_in.1, s32[16,8,256]{2,1,0:T(8,128)} %mat_in.1, f32[8]{0:T(128)} %eps_in.1, f32[8]{0:T(128)} %sig_in.1), custom_call_target="tpu_custom_call" | custom-call | tf_op jit(solution)/shard_map/pallas_call | solution.py:496
  20.5 0.0 copy-start
  20.5 1.8 %copy.9 = f32[3,16,8,256]{3,2,1,0:T(8,128)} copy(f32[3,16,8,256]{3,2,1,0:T(8,128)} %get-tuple-element.4) | data formatting | bytes 786432
  22.3 0.0 copy-done
  22.3 0.7 %copy.10 = f32[3,16,8,256]{3,2,1,0:T(8,128)} copy(f32[3,16,8,256]{3,2,1,0:T(8,128)S(1)} %copy-done) | data formatting | bytes 786432
Async XLA Ops:
  20.5 1.8 %copy-start = (f32[3,16,8,256]{3,2,1,0:T(8,128)S(1)}, f32[3,16,8,256]{3,2,1,0:T(8,128)}, u32[]{:S(2)}) copy-start(f32[3,16,8,256]{3,2,1,0:T(8,128)} %get-tuple-element.5) | copy-start | bytes 1179652
